TPU v7x, 32 devices: a whole 2x2x4 slice. The times are simulated.
32 devices in a mesh: parts: 2 (over x), leaf: 16 (over z, y, core).
Axes of the slice: x: 2, y: 2, z: 4, core: 2. Of those that a mesh axis runs over, the one named last changes fastest.
Arguments:
- krylov: float32 [8, 131072], P(None, ('parts', 'leaf')), parts along dimension 1, may hold values from -6 to 6
- tree_perm: int32 [131072], P(('parts', 'leaf')), parts along dimension 0, may hold values from 0 to 4095, as said below
- owner: int32 [512], P('parts'), parts along dimension 0, may hold values from 0 to 255, as said below
- near_src: int32 [1024], P(('parts', 'leaf')), parts along dimension 0, may hold values from -1 to 255, as said below
- near_tgt: int32 [1024], P(('parts', 'leaf')), parts along dimension 0, may hold values from 0 to 15
- near_blocks: float32 [1024, 256, 256], P(('parts', 'leaf')), parts along dimension 0, may hold values from -0.375 to 0.375
- basis: float32 [32, 131072], P(None, ('parts', 'leaf')), parts along dimension 1, may hold values from -0.375 to 0.375
- transfer: float32 [32, 16384], P(None, ('parts', 'leaf')), parts along dimension 1, may hold values from -0.25 to 0.25
- top_coup: float32 [1024, 512], P(('parts', 'leaf')), parts along dimension 0, may hold values from -0.25 to 0.25
- far_src: int32 [2048], P(('parts', 'leaf')), parts along dimension 0, may hold values from 0 to 255
- far_coup: float32 [32, 65536], P(None, ('parts', 'leaf')), parts along dimension 1, may hold values from -0.5 to 0.5
Outputs:
- next_vector: float32 [131072], P(('parts', 'leaf')), parts along dimension 0
- coeffs: float32 [18], P('parts'), parts along dimension 0
There are 2 independent parts, one for each index of `parts`. A program takes and returns all parts, laid end to end along the dimension named above; each array names one. Nothing has to cross between parts.
Inputs may be any that keep to these rules, and one draw needn't show every extreme that they name: `tree_perm`: each device's block of 4096 entries is a permutation of 0 to 4095. `owner`: A permutation of 0 to 255. `near_src`: on device d, slots g * 8 to (g + 1) * 8 - 1 name leaves stored (by owner) on device (d + s_g) mod 16, with s = (0, -1, 1, -2) for g = 0, 1, 2, 3. Live slots of a device come first, at least 8 of them; some device has all 32 live.
All inputs are finite; a program needn't handle non-finite values.
Results may differ from a plain program's by a relative error of at most 0.000061.
Values sent between devices are 32-bit elements; how exact they have to be, the bound alone decides.
A program may use at most 64 MiB of HBM per device.

v0:
```python
import jax
import jax.numpy as jnp
from jax import lax
from jax.sharding import PartitionSpec as P

M = 256
K = 32
CAP = 8
NF = 4
J = 8


HI = lax.Precision.HIGHEST


def from_behind(block, axis, distance):
    devices = range(lax.axis_size(axis))
    route = [((i - distance) % len(devices), i) for i in devices]
    return lax.ppermute(block, axis, route)


def on_device(
    krylov,
    tree_perm,
    owner,
    near_src,
    near_tgt,
    near_blocks,
    basis,
    transfer,
    top_coup,
    far_src,
    far_coup,
):
    ndev = lax.axis_size("leaf")
    local_rows = tree_perm.shape[0]
    leaves = local_rows // M
    total = float(local_rows * ndev)
    x = krylov[J - 1]
    xc = jnp.take(x, tree_perm)
    xleaf = xc.reshape(leaves, M)
    bases = basis.reshape(K, leaves, M)
    coef = jnp.einsum("kcm,cm->ck", bases, xleaf, precision=HI)
    trans = transfer.reshape(K, leaves, K)
    parent = jnp.einsum("acb,cb->a", trans, coef, precision=HI)
    coef_all, parent_all = (
        lax.all_gather(coef.reshape(leaves * K), "leaf", axis=0, tiled=True),
        lax.all_gather(parent, "leaf", axis=0, tiled=True),
    )
    me = lax.axis_index("leaf")
    keep = (jnp.arange(ndev, dtype=jnp.int32) != me).astype(jnp.float32)
    top = top_coup.reshape(K, ndev, K)
    field_top = jnp.einsum("aeb,e,eb->a", top, keep, parent_all.reshape(ndev, K), precision=HI)
    field = jnp.einsum("acb,a->cb", trans, field_top, precision=HI)
    far_rows = coef_all.reshape(ndev * leaves, K)[owner[far_src]].reshape(leaves, NF, K)
    field = field + jnp.einsum(
        "acfb,cfb->ca", far_coup.reshape(K, leaves, NF, K), far_rows, precision=HI
    )
    yc = jnp.einsum("kcm,ck->cm", bases, field, precision=HI)
    live = near_src >= 0
    slots = owner[jnp.maximum(near_src, 0)]
    src_loc = slots % leaves
    wanted = jnp.where(live, src_loc, -1).reshape(4, CAP)
    pieces = [xleaf[jnp.maximum(wanted[0], 0)]]
    for group, distance in ((1, 1), (2, -1), (3, 2)):
        nearby = from_behind(xleaf, "leaf", distance)
        pieces.append(nearby[jnp.maximum(wanted[group], 0)])
    src_rows = jnp.concatenate(pieces, axis=0)
    contrib = jnp.einsum("nab,nb->na", near_blocks, src_rows, precision=HI)
    contrib = contrib * live[:, None].astype(jnp.float32)
    onehot = (near_tgt[None, :] == jnp.arange(leaves, dtype=jnp.int32)[:, None]).astype(jnp.float32)
    yc = yc + jnp.dot(onehot, contrib, precision=HI)
    y = jnp.zeros((local_rows,), jnp.float32).at[tree_perm].set(yc.reshape(local_rows))
    w = 0.5 * x + y
    h = lax.psum(jnp.dot(krylov, w, precision=HI), "leaf") / total
    wp = w - jnp.dot(h, krylov, precision=HI)
    squares = lax.psum(jnp.sum(wp * wp), "leaf") / total
    beta = jnp.sqrt(squares + 1e-06)
    return (wp / beta, jnp.concatenate([h, beta[None]]))


def solution(mesh):
    return jax.shard_map(
        on_device,
        mesh=mesh,
        in_specs=(
            P(None, ("parts", "leaf")),
            P(("parts", "leaf")),
            P("parts"),
            P(("parts", "leaf")),
            P(("parts", "leaf")),
            P(("parts", "leaf"), None, None),
            P(None, ("parts", "leaf")),
            P(None, ("parts", "leaf")),
            P(("parts", "leaf"), None),
            P(("parts", "leaf")),
            P(None, ("parts", "leaf")),
        ),
        out_specs=(P(("parts", "leaf")), P("parts")),
        check_vma=False,
    )
```

profile of v0, /device:TPU:0, one launch (start us, length us, event | category | flops | bytes accessed | tf_op | source)
XLA Modules:
  0.0 182.9 jit_solution(8190561430735265074)
XLA Ops:
  0.6 0.7 broadcast_clamp_fusion
  1.4 0.9 slice.19
  2.4 23.0 %gather_fusion = f32[4096]{0:T(1024)S(1)} fusion(f32[4096]{0:T(1024)S(1)} %bitcast.73, s32[4096]{0:T(1024)S(1)} %get-tuple-element.4), kind=kCustom, calls=%fused_computation | custom fusion | bytes 49152 | tf_op jit(solution)/shard_map/jit(_take)/gather | solution.py:40
  25.5 3.0 %collective-permute-start.2 = (f32[16,256]{1,0:T(8,128)S(1)}, f32[16,256]{1,0:T(8,128)S(1)}, u32[]{:S(2)}, u32[]{:S(2)}) collective-permute-start(f32[16,256]{1,0:T(8,128)S(1)} %select_n.45), channel_id=1, source_target_pairs={{14,0},{15,1},{0,2},{1,3},{2,4},{3,5},{4,6},{5,7},{6,8},{7,9},{8,1... | collective-permute-start | bytes 49160 | tf_op jit(solution)/shard_map/ppermute | solution.py:19
  28.5 2.5 %collective-permute-start.1 = (f32[16,256]{1,0:T(8,128)S(1)}, f32[16,256]{1,0:T(8,128)S(1)}, u32[]{:S(2)}, u32[]{:S(2)}) collective-permute-start(f32[16,256]{1,0:T(8,128)S(1)} %select_n.45), channel_id=1, source_target_pairs={{1,0},{2,1},{3,2},{4,3},{5,4},{6,5},{7,6},{8,7},{9,8},{10,9},{11,1... | collective-permute-start | bytes 49160 | tf_op jit(solution)/shard_map/ppermute | solution.py:19
  31.1 0.7 gather_fusion.3
  32.0 0.5 fusion.3
  32.9 0.6 dynamic-slice
  34.4 33.9 %all-reduce = f32[512]{0:T(512)S(1)} all-reduce(f32[512]{0:T(512)S(1)} %dynamic-update-slice), channel_id=1, replica_groups=mesh['parts'=2,'leaf'=16] {'leaf'}, use_global_device_ids=true, to_apply=%add | all-reduce | flops 512 | bytes 4096
  69.3 17.2 %all-gather = f32[16,1,512]{2,1,0:T(1,128)S(1)} all-gather(f32[1,1,512]{2,1,0:T(1,128)S(1)} %reshape.166), channel_id=1, replica_groups=mesh['parts'=2,'leaf'=16] {'leaf'}, dimensions={0}, use_global_device_ids=true | all-gather | bytes 34816 | tf_op jit(solution)/shard_map/all_gather | solution.py:47
  86.7 0.8 gather_fusion.1
  87.9 0.6 gather_fusion.2
  88.5 1.0 fusion.22
  89.9 0.6 gather_fusion.4
  90.5 0.6 gather_fusion.7
  91.1 0.6 gather_fusion.6
  91.7 0.6 gather_fusion.5
  92.2 10.2 %fusion.11 = f32[32,1,256]{2,1,0:T(1,128)S(1)} fusion(f32[32,256,256]{2,1,0:T(8,128)} %param.16, f32[32,256,1]{1,0,2:T(8,128)S(1)} %maximum_bitcast_fusion), kind=kOutput, calls=%fused_computation.27 | convolution fusion | flops 25165824 | bytes 8454144 | tf_op jit(solution)/shard_map/nab,nb->na/dot_general | solution.py:69
  102.7 15.5 %scatter_custom_fusion = f32[4096]{0:T(1024)S(1)} fusion(s32[4096]{0:T(1024)S(1)} %get-tuple-element.5, f32[4096]{0:T(1024)S(1)} %bitcast.88, f32[]{:T(128)} %constant.23.clone.1), kind=kCustom, calls=%fused_computation.37 | custom fusion | bytes 16388 | tf_op jit(solution)/shard_map/scatter | solution.py:73
  118.6 31.4 %psum.14 = f32[8]{0:T(128)S(1)} all-reduce(f32[8]{0:T(128)S(1)} %convolution_bitcast_fusion), channel_id=1, replica_groups=mesh['parts'=2,'leaf'=16] {'leaf'}, use_global_device_ids=true, to_apply=%region_1.2 | all-reduce | flops 8 | bytes 64 | tf_op jit(solution)/shard_map/psum | solution.py:75
  150.3 0.6 multiply_reduce_fusion
  150.9 30.1 %psum.15 = f32[]{:T(128)} all-reduce(f32[]{:T(128)} %get-tuple-element.2), channel_id=1, replica_groups=mesh['parts'=2,'leaf'=16] {'leaf'}, use_global_device_ids=true, to_apply=%region_3.4 | all-reduce | flops 1 | bytes 8 | tf_op jit(solution)/shard_map/psum | solution.py:77
  181.7 0.6 broadcast_divide_fusion
  182.3 0.6 pad_maximum_fusion
  (62 shorter events, 3.6 us)
Async XLA Ops:
  0.6 30.5 %copy-start = (s32[256]{0:T(256)S(1)}, s32[256]{0:T(256)}, u32[]{:S(2)}) copy-start(s32[256]{0:T(256)} %param.13) | copy-start | bytes 3076
  2.3 23.1 %copy-start.6 = (s32[4096]{0:T(1024)S(1)}, s32[4096]{0:T(1024)}, u32[]{:S(2)}) copy-start(s32[4096]{0:T(1024)} %param.12) | copy-start | bytes 49156
  2.3 28.8 %copy-start.8 = (s32[32]{0:T(128)S(1)}, s32[32]{0:T(128)}, u32[]{:S(2)}) copy-start(s32[32]{0:T(128)} %param.14) | copy-start | bytes 388
  2.3 29.6 %copy-start.4 = (f32[32,512]{1,0:T(8,128)S(1)}, f32[32,512]{1,0:T(8,128)}, u32[]{:S(2)}) copy-start(f32[32,512]{1,0:T(8,128)} %param.18) | copy-start | bytes 196612
  2.3 29.7 %copy-start.1 = (f32[32,4096]{1,0:T(8,128)S(1)}, f32[32,4096]{1,0:T(8,128)}, u32[]{:S(2)}) copy-start(f32[32,4096]{1,0:T(8,128)} %param.17) | copy-start | bytes 1572868
  2.3 30.6 %copy-start.10 = (u32[32]{0:T(128)S(1)}, u32[32]{0:T(128)}, u32[]{:S(2)}) copy-start(u32[32]{0:T(128)} %constant.64) | copy-start | bytes 388
  2.4 66.1 %copy-start.5 = (f32[32,512]{1,0:T(8,128)S(1)}, f32[32,512]{1,0:T(8,128)}, u32[]{:S(2)}) copy-start(f32[32,512]{1,0:T(8,128)} %param.19) | copy-start | bytes 196612
  2.4 84.3 %copy-start.9 = (s32[64]{0:T(128)S(1)}, s32[64]{0:T(128)}, u32[]{:S(2)}) copy-start(s32[64]{0:T(128)} %param.20) | copy-start | bytes 772
  2.4 85.1 %copy-start.3 = (f32[32,2048]{1,0:T(8,128)S(1)}, f32[32,2048]{1,0:T(8,128)}, u32[]{:S(2)}) copy-start(f32[32,2048]{1,0:T(8,128)} %param.21) | copy-start | bytes 786436
  25.4 77.0 %copy-start.7 = (s32[32]{0:T(128)S(1)}, s32[32]{0:T(128)}, u32[]{:S(2)}) copy-start(s32[32]{0:T(128)} %param.15) | copy-start | bytes 388
  25.5 92.8 %copy-start.2 = (f32[8,4096]{1,0:T(8,128)S(1)}, f32[8,4096]{1,0:T(8,128)}, u32[]{:S(2)}) copy-start(f32[8,4096]{1,0:T(8,128)} %param.11) | copy-start | bytes 393220
  25.5 65.0 %collective-permute-start.2 = (f32[16,256]{1,0:T(8,128)S(1)}, f32[16,256]{1,0:T(8,128)S(1)}, u32[]{:S(2)}, u32[]{:S(2)}) collective-permute-start(f32[16,256]{1,0:T(8,128)S(1)} %select_n.45), channel_id=1, source_target_pairs={{14,0},{15,1},{0,2},{1,3},{2,4},{3,5},{4,6},{5,7},{6,8},{7,9},{8,1... | collective-permute-start | bytes 49160 | tf_op jit(solution)/shard_map/ppermute | solution.py:19
  28.5 62.5 %collective-permute-start.1 = (f32[16,256]{1,0:T(8,128)S(1)}, f32[16,256]{1,0:T(8,128)S(1)}, u32[]{:S(2)}, u32[]{:S(2)}) collective-permute-start(f32[16,256]{1,0:T(8,128)S(1)} %select_n.45), channel_id=1, source_target_pairs={{1,0},{2,1},{3,2},{4,3},{5,4},{6,5},{7,6},{8,7},{9,8},{10,9},{11,1... | collective-permute-start | bytes 49160 | tf_op jit(solution)/shard_map/ppermute | solution.py:19
  31.1 60.6 %collective-permute-start = (f32[16,256]{1,0:T(8,128)S(1)}, f32[16,256]{1,0:T(8,128)S(1)}, u32[]{:S(2)}, u32[]{:S(2)}) collective-permute-start(f32[16,256]{1,0:T(8,128)S(1)} %select_n.45), channel_id=1, source_target_pairs={{15,0},{0,1},{1,2},{2,3},{3,4},{4,5},{5,6},{6,7},{7,8},{8,9},{9,10... | collective-permute-start | bytes 49160 | tf_op jit(solution)/shard_map/ppermute | solution.py:19
where the time goes:
time: 183 us
  blocking collectives  113 us (62%)
  local copies, waits for them, and re-layouts  45.6 us (25%)
  matrix products  13.9 us (8%)
  starting transfers between devices  5.57 us (3%)
  other arithmetic  2.85 us (2%)
  between operations  2.35 us (1%)
    unnamed x1, blocking collectives  33.9 us
    psum x1, blocking collectives, on_device(): h = lax.psum(jnp.dot(krylov, w, precision=HI), 'leaf') / total  31.4 us
    psum x1, blocking collectives, on_device(): squares = lax.psum(jnp.sum(wp * wp), 'leaf') / total  30.1 us
    gather x1, local copies, waits for them, and re-layouts, on_device(): xc = jnp.take(x, tree_perm)  23 us
    all_gather x1, blocking collectives, on_device(): lax.all_gather(coef.reshape(leaves * K), 'leaf', axis=0, tiled=True)  17.2 us
    scatter x1, local copies, waits for them, and re-layouts, on_device(): jnp.zeros((local_rows,), jnp.float32).at[tree_perm]  15.5 us
    dot_general x1, matrix products, on_device(): contrib = jnp.einsum('nab,nb->na', near_blocks, src_rows, precision=HI)  10.2 us
    ppermute x3, starting transfers between devices, from_behind(): return lax.ppermute(block, axis, route)  5.57 us
  transfers between devices with their start and end apart: 3, of which 0 were waited for; matrix products, arithmetic and copies ran while one was open for 5% of the time, Pallas kernels for 0%

commit v1 on v0

v1 whole, which is shorter than its diff:
```python
import functools

import jax
import jax.numpy as jnp
from jax import lax
from jax.experimental import pallas as pl
from jax.experimental.pallas import tpu as pltpu
from jax.sharding import PartitionSpec as P

M = 256
K = 32
CAP = 8
NF = 4
J = 8
LANES = 128
MESH = pl.DeviceIdType.MESH
F32 = jnp.float32
BF16 = jnp.bfloat16


def iota(shape, dim):
    return lax.broadcasted_iota(jnp.int32, shape, dim)


def split3(v):
    a = v.astype(BF16)
    r = v - a.astype(F32)
    b = r.astype(BF16)
    c = (r - b.astype(F32)).astype(BF16)
    return a, b, c


def rowsum(v):
    return jnp.sum(v, axis=0, keepdims=True)


def lanesum(v):
    return jnp.sum(v, axis=1, keepdims=True)


def kernel(
    ndev, leaves, total,
    kry_h, perm_h, basis_h, trans_h, top_h, far_h, nb_h,
    owner_s, nsrc_s, ntgt_s, fsrc_s,
    out_ref, coef_ref,
    kry, perm, basis, trans, top, far, nb,
    x32, oh, xown, xin1, xin2, xin3, land1, land2, rolled, idx, ybuf,
    lsem, nsem, xsend, xrecv, s1, r1, s2, r2,
):
    me = lax.axis_index("leaf")
    chunks = leaves * 2
    groups = leaves // 4

    def peer(k):
        return {"leaf": lax.rem(me + k, ndev)}

    def local(i, src, dst):
        return pltpu.make_async_copy(src, dst, lsem.at[i])

    loads = [
        local(i, s, d)
        for i, (s, d) in enumerate(
            ((kry_h, kry), (perm_h, perm), (basis_h, basis), (trans_h, trans), (top_h, top), (far_h, far))
        )
    ]
    near = [
        pltpu.make_async_copy(nb_h.at[pl.ds(g * CAP, CAP)], nb.at[pl.ds(g * CAP, CAP)], nsem.at[g])
        for g in range(4)
    ]
    for cp in loads[:4]:
        cp.start()
    barrier = pltpu.get_barrier_semaphore()

    def greet(k, _):
        pl.semaphore_signal(barrier, inc=1, device_id=peer(k), device_id_type=MESH)
        return 0

    lax.fori_loop(1, ndev, greet, 0)
    for cp in near:
        cp.start()
    for cp in loads[4:]:
        cp.start()

    sub8 = iota((8, LANES), 0)
    lane8 = iota((8, LANES), 1)
    sub32 = iota((K, LANES), 0)
    lane32 = iota((K, LANES), 1)
    lane1 = iota((1, LANES), 1)

    loads[1].wait()
    sub128 = iota((LANES, LANES), 0)
    for i in range(chunks):
        lo = perm[i : i + 1, :] & (LANES - 1)
        oh[:, i * LANES : (i + 1) * LANES] = jnp.where(sub128 == lo, 1.0, 0.0).astype(BF16)
    loads[0].wait()
    for i in range(chunks):
        x32[i : i + 1, :] = kry[J - 1 : J, i * LANES : (i + 1) * LANES]
    x3 = jnp.concatenate(split3(x32[...]), axis=0)
    for i in range(chunks):
        a = jnp.dot(x3, oh[:, i * LANES : (i + 1) * LANES], preferred_element_type=F32)
        a = a[:chunks] + a[chunks : 2 * chunks] + a[2 * chunks :]
        hi = perm[i : i + 1, :] >> 7
        half = (i % 2) * LANES
        xown[i // 2 : i // 2 + 1, half : half + LANES] = rowsum(jnp.where(iota((chunks, LANES), 0) == hi, a, 0.0))

    pl.semaphore_wait(barrier, ndev - 1)

    xbufs = (xown, xin1, xin2, xin3)
    xcopies = [
        pltpu.make_async_remote_copy(
            src_ref=xown,
            dst_ref=xbufs[g],
            send_sem=xsend.at[g],
            recv_sem=xrecv.at[g],
            device_id=peer(hop + ndev),
            device_id_type=MESH,
        )
        for g, hop in ((1, 1), (2, -1), (3, 2))
    ]
    for cp in xcopies:
        cp.start()

    loads[2].wait()
    loads[3].wait()
    tile = jnp.zeros((8, LANES), F32)
    qacc = jnp.zeros((K, LANES), F32)
    for t in range(groups):
        acc = jnp.zeros((K, LANES), F32)
        for cc in range(4):
            c = 4 * t + cc
            p = (
                basis[:, c * M : c * M + LANES] * xown[c : c + 1, :LANES]
                + basis[:, c * M + LANES : (c + 1) * M] * xown[c : c + 1, LANES:]
            )
            acc = acc + jnp.where(lane32 == cc * K + sub32, lanesum(p), 0.0)
        row = rowsum(acc)
        qacc = qacc + trans[:, t * LANES : (t + 1) * LANES] * row
        tile = jnp.where(sub8 == t, row, tile)
    qrow = rowsum(jnp.where(lane32 % K == sub32, lanesum(qacc), 0.0))
    land1[me] = jnp.where(sub8 == groups, qrow, tile)

    def send1(k):
        return pltpu.make_async_remote_copy(
            src_ref=land1.at[me],
            dst_ref=land1.at[me],
            send_sem=s1.at[k],
            recv_sem=r1.at[k],
            device_id=peer(k),
            device_id_type=MESH,
        )

    def recv1(k):
        src = lax.rem(me - k + ndev, ndev)
        return pltpu.make_async_remote_copy(
            src_ref=land1.at[src],
            dst_ref=land1.at[src],
            send_sem=s1.at[k],
            recv_sem=r1.at[k],
            device_id=peer(k),
            device_id_type=MESH,
        )

    def start1(k, _):
        send1(k).start()
        return 0

    lax.fori_loop(1, ndev, start1, 0)

    rows = iota((leaves, M), 0)
    sub16 = iota((16, M), 0)
    yc = jnp.zeros((leaves, M), F32)
    for g in range(4):
        near[g].wait()
        if g:
            xcopies[g - 1].wait_recv()

        def slot(i, yc):
            n = g * CAP + i
            src = nsrc_s[n]
            loc = lax.rem(owner_s[jnp.maximum(src, 0)], leaves)
            x = xbufs[g][pl.ds(loc, 1), :]
            xh = x.astype(BF16).astype(F32)
            lhs = jnp.where(sub16 == 0, xh, jnp.where(sub16 == 1, x - xh, 0.0)).astype(BF16)
            blk = nb[n]
            bh = blk.astype(BF16)
            bl = (blk - bh.astype(F32)).astype(BF16)
            dims = (((1,), (1,)), ((), ()))
            r = lax.dot_general(lhs, bh, dims, preferred_element_type=F32)
            r = r + lax.dot_general(lhs, bl, dims, preferred_element_type=F32)
            tgt = jnp.where(src >= 0, ntgt_s[n], -1)
            return yc + jnp.where(rows == tgt, r[0:1] + r[1:2], 0.0)

        yc = lax.fori_loop(0, CAP, slot, yc, unroll=True)

    gram = jnp.zeros((8, LANES), F32)
    for k in range(J):
        acc = jnp.zeros((8, LANES), F32)
        for i in range(chunks):
            part = kry[:, i * LANES : (i + 1) * LANES]
            acc = acc + part * kry[k : k + 1, i * LANES : (i + 1) * LANES]
        gram = gram + jnp.where(lane8 % J == k, lanesum(acc), 0.0)
    message = jnp.where(lane8 // J == sub8, gram, 0.0)

    stride = ndev * 8
    for i in range(leaves * NF):
        s = owner_s[fsrc_s[i]]
        c = lax.rem(s, leaves)
        turn = (i % NF - c) & 3
        idx[i] = turn * stride + (s // leaves) * 8 + c // 4

    def wait1(k, _):
        recv1(k).wait_recv()
        return 0

    lax.fori_loop(1, ndev, wait1, 0)

    got = land1[...].reshape(stride, LANES)
    rolled[0:stride, :] = got
    for s in range(1, 4):
        rolled[s * stride : (s + 1) * stride, :] = pltpu.roll(got, K * s, 1)
    loads[4].wait()
    loads[5].wait()
    gacc = jnp.zeros((K, LANES), F32)
    for t in range(ndev // 4):
        row = jnp.zeros((1, LANES), F32)
        for ee in range(4):
            e = 4 * t + ee
            row = row + jnp.where((lane1 // K == ee) & (me != e), land1[e, groups : groups + 1, :], 0.0)
        gacc = gacc + top[:, t * LANES : (t + 1) * LANES] * row
    gcol = lanesum(gacc)

    y3 = jnp.zeros((3 * chunks, LANES), F32)
    for c in range(leaves):
        t, cc = c // 4, c % 4
        if cc == 0:
            grow = rowsum(trans[:, t * LANES : (t + 1) * LANES] * gcol)
        r = jnp.zeros((1, LANES), F32)
        for f in range(NF):
            r = jnp.where(lane1 // K == f, rolled[pl.ds(idx[c * NF + f], 1), :], r)
        acc = far[:, c * LANES : (c + 1) * LANES] * r + jnp.where(lane32 == cc * K + sub32, grow, 0.0)
        g = lanesum(acc)
        for half in range(2):
            i = 2 * c + half
            yrow = yc[c : c + 1, half * LANES : (half + 1) * LANES] + rowsum(basis[:, i * LANES : (i + 1) * LANES] * g)
            hit = iota((chunks, LANES), 0) == perm[i : i + 1, :] >> 7
            lhs = jnp.concatenate([jnp.where(hit, v.astype(F32), 0.0).astype(BF16) for v in split3(yrow)], axis=0)
            y3 = y3 + lax.dot_general(
                lhs, oh[:, i * LANES : (i + 1) * LANES], (((1,), (1,)), ((), ())), preferred_element_type=F32
            )
    y = y3[:chunks] + y3[chunks : 2 * chunks] + y3[2 * chunks :]
    ybuf[...] = y

    acc = jnp.zeros((8, LANES), F32)
    sq = jnp.zeros((8, LANES), F32)
    for i in range(chunks):
        acc = acc + kry[:, i * LANES : (i + 1) * LANES] * ybuf[i : i + 1, :]
    for i in range(chunks // 8):
        sq = sq + ybuf[8 * i : 8 * i + 8, :] * ybuf[8 * i : 8 * i + 8, :]
    message = message + jnp.where(lane8 == 64 + sub8, lanesum(acc), 0.0)
    message = message + jnp.where(lane8 == 72, lanesum(sq), 0.0)
    land2[me] = rowsum(message)

    def send2(k):
        return pltpu.make_async_remote_copy(
            src_ref=land2.at[me],
            dst_ref=land2.at[me],
            send_sem=s2.at[k],
            recv_sem=r2.at[k],
            device_id=peer(k),
            device_id_type=MESH,
        )

    def recv2(k):
        src = lax.rem(me - k + ndev, ndev)
        return pltpu.make_async_remote_copy(
            src_ref=land2.at[src],
            dst_ref=land2.at[src],
            send_sem=s2.at[k],
            recv_sem=r2.at[k],
            device_id=peer(k),
            device_id_type=MESH,
        )

    def start2(k, _):
        send2(k).start()
        return 0

    def wait2(k, _):
        recv2(k).wait_recv()
        return 0

    lax.fori_loop(1, ndev, start2, 0)
    for cp in xcopies:
        cp.wait_send()

    def sent1(k, _):
        send1(k).wait_send()
        return 0

    lax.fori_loop(1, ndev, sent1, 0)
    lax.fori_loop(1, ndev, wait2, 0)

    sums = land2[0]
    for e in range(1, ndev):
        sums = sums + land2[e]
    ky = lanesum(jnp.where(lane8 == 64 + sub8, sums, 0.0))
    kx = lanesum(jnp.where(lane8 == (J - 1) * J + sub8, sums, 0.0))
    h = (0.5 * kx + ky) * (1.0 / total)
    is_x = iota((8, 1), 0) == J - 1
    d = h - jnp.where(is_x, 0.5, 0.0)
    left = rowsum(jnp.where(lane8 // J == sub8, d, 0.0))
    right = rowsum(jnp.where(lane8 % J == sub8, d, 0.0))
    along = rowsum(jnp.where(lane8 == 64 + sub8, -2.0 * d, 0.0))
    terms = sums * (left * right + along + jnp.where(lane1 == 72, 1.0, 0.0))
    squares = jnp.maximum(lanesum(terms), 0.0) * (1.0 / total)
    beta = jnp.sqrt(squares + 1e-06)
    coef_ref[...] = (rowsum(jnp.where(lane8 == sub8, h, 0.0)) + jnp.where(lane1 == J, beta, 0.0))[:, : J + 1]
    for i in range(chunks):
        out_ref[i : i + 1, :] = (ybuf[i : i + 1, :] - rowsum(kry[:, i * LANES : (i + 1) * LANES] * d)) / beta

    def sent2(k, _):
        send2(k).wait_send()
        return 0

    lax.fori_loop(1, ndev, sent2, 0)


def on_device(
    krylov,
    tree_perm,
    owner,
    near_src,
    near_tgt,
    near_blocks,
    basis,
    transfer,
    top_coup,
    far_src,
    far_coup,
):
    ndev = lax.axis_size("leaf")
    local_rows = tree_perm.shape[0]
    leaves = local_rows // M
    chunks = local_rows // LANES
    hbm = pl.BlockSpec(memory_space=pl.ANY)
    smem = pl.BlockSpec(memory_space=pltpu.SMEM)
    vmem = pl.BlockSpec(memory_space=pltpu.VMEM)
    arrays = (krylov, tree_perm.reshape(chunks, LANES), basis, transfer, top_coup, far_coup, near_blocks)
    dma = pltpu.SemaphoreType.DMA
    nxt, coeffs = pl.pallas_call(
        functools.partial(kernel, ndev, leaves, float(local_rows * ndev)),
        out_shape=(
            jax.ShapeDtypeStruct((chunks, LANES), F32),
            jax.ShapeDtypeStruct((1, J + 1), F32),
        ),
        in_specs=[hbm] * 7 + [smem] * 4,
        out_specs=(vmem, vmem),
        scratch_shapes=[pltpu.VMEM(a.shape, a.dtype) for a in arrays]
        + [
            pltpu.VMEM((chunks, LANES), F32),
            pltpu.VMEM((LANES, local_rows), BF16),
            pltpu.VMEM((leaves, M), F32),
            pltpu.VMEM((leaves, M), F32),
            pltpu.VMEM((leaves, M), F32),
            pltpu.VMEM((leaves, M), F32),
            pltpu.VMEM((ndev, 8, LANES), F32),
            pltpu.VMEM((ndev, 1, LANES), F32),
            pltpu.VMEM((4 * ndev * 8, LANES), F32),
            pltpu.SMEM((leaves * NF,), jnp.int32),
            pltpu.VMEM((chunks, LANES), F32),
            dma((6,)),
            dma((4,)),
            dma((4,)),
            dma((4,)),
            dma((ndev,)),
            dma((ndev,)),
            dma((ndev,)),
            dma((ndev,)),
        ],
        compiler_params=pltpu.CompilerParams(
            collective_id=0, has_side_effects=True, vmem_limit_bytes=40 * 1024 * 1024
        ),
        cost_estimate=pl.CostEstimate(flops=20_000_000, bytes_accessed=10_000_000, transcendentals=0),
    )(*arrays, owner, near_src, near_tgt, far_src)
    return nxt.reshape(local_rows), coeffs.reshape(J + 1)


def solution(mesh):
    return jax.shard_map(
        on_device,
        mesh=mesh,
        in_specs=(
            P(None, ("parts", "leaf")),
            P(("parts", "leaf")),
            P("parts"),
            P(("parts", "leaf")),
            P(("parts", "leaf")),
            P(("parts", "leaf"), None, None),
            P(None, ("parts", "leaf")),
            P(None, ("parts", "leaf")),
            P(("parts", "leaf"), None),
            P(("parts", "leaf")),
            P(None, ("parts", "leaf")),
        ),
        out_specs=(P(("parts", "leaf")), P("parts")),
        check_vma=False,
    )
```

time: 183 us -> 32.8 us (0.18)
  blocking collectives: 113 us -> 0 us
  local copies, waits for them, and re-layouts: 45.6 us -> 12.4 us
  Pallas kernels: 0 us -> 19.2 us
  matrix products: 13.9 us -> 0 us
  starting transfers between devices: 5.57 us -> 0 us
  other arithmetic: 2.85 us -> 0 us
    psum x2 -> x0, blocking collectives: 61.5 us -> none  [the longest x1 31.4 us: on_device(): h = lax.psum(jnp.dot(krylov, w, precision=HI), 'leaf') / total]
    unnamed x1 -> x0, blocking collectives: 33.9 us -> none
    gather x8 -> x0, local copies, waits for them, and re-layouts: 27.4 us -> none  [the longest x1 23 us: on_device(): xc = jnp.take(x, tree_perm)]
    pallas_call x0 -> x1, Pallas kernels: none -> 19.2 us  [on_device(): pl.pallas_call(functools.partial(kernel, ndev, leaves, float(local_rows *...]
    all_gather x1 -> x0, blocking collectives: 17.2 us -> none  [on_device(): lax.all_gather(coef.reshape(leaves * K), 'leaf', axis=0, tiled=True)]
    scatter x1 -> x0, local copies, waits for them, and re-layouts: 15.5 us -> none  [on_device(): jnp.zeros((local_rows,), jnp.float32).at[tree_perm]]
    dot_general x10 -> x0, matrix products: 13.9 us -> none  [the longest x1 10.2 us: on_device(): contrib = jnp.einsum('nab,nb->na', near_blocks, src_rows, precision=HI)]
    unnamed x27 -> x24, local copies, waits for them, and re-layouts: 1.07 us -> 12.4 us
  transfers between devices with their start and end apart: 3 -> 0, of which waited for: 0 -> 0; matrix products, arithmetic and copies ran while one was open for 5% -> 0% of each run, Pallas kernels for 0% -> 0%
where the time goes in v1:
time: 32.8 us; the launch traced here: 32.3 us
  Pallas kernels  19.2 us (59%)
  local copies, waits for them, and re-layouts  12.4 us (38%)
  between operations  0.66 us (2%)
    pallas_call x1, Pallas kernels, on_device(): pl.pallas_call(functools.partial(kernel, ndev, leaves, float(local_rows *...  19.2 us
    unnamed x24, local copies, waits for them, and re-layouts  12.4 us

profile of v1, /device:TPU:0, one launch (start us, length us, event | category | flops | bytes accessed | tf_op | source)
XLA Modules:
  0.0 32.3 jit_solution(5772446504001394683)
XLA Ops:
  0.6 0.0 copy-start
  0.6 3.4 %copy-done = f32[32,256,256]{2,1,0:T(8,128)S(1)} copy-done((f32[32,256,256]{2,1,0:T(8,128)S(1)}, f32[32,256,256]{2,1,0:T(8,128)}, u32[]{:S(2)}) %copy-start) | copy-done | bytes 8388632
  4.0 0.0 copy-start.1
  4.0 1.0 %copy-done.1 = f32[32,4096]{1,0:T(8,128)S(1)} copy-done((f32[32,4096]{1,0:T(8,128)S(1)}, f32[32,4096]{1,0:T(8,128)}, u32[]{:S(2)}) %copy-start.1) | copy-done | bytes 524312
  5.1 0.0 copy-start.2
  5.1 0.9 %copy-done.2 = f32[32,2048]{1,0:T(8,128)S(1)} copy-done((f32[32,2048]{1,0:T(8,128)S(1)}, f32[32,2048]{1,0:T(8,128)}, u32[]{:S(2)}) %copy-start.2) | copy-done | bytes 262168
  6.0 0.0 copy-start.3
  6.0 0.9 %copy-done.3 = f32[8,4096]{1,0:T(8,128)S(1)} copy-done((f32[8,4096]{1,0:T(8,128)S(1)}, f32[8,4096]{1,0:T(8,128)}, u32[]{:S(2)}) %copy-start.3) | copy-done | bytes 131096
  6.9 0.0 copy-start.4
  6.9 0.8 %copy-done.4 = f32[32,512]{1,0:T(8,128)S(1)} copy-done((f32[32,512]{1,0:T(8,128)S(1)}, f32[32,512]{1,0:T(8,128)}, u32[]{:S(2)}) %copy-start.4) | copy-done | bytes 65560
  7.8 0.0 copy-start.5
  7.8 0.8 %copy-done.5 = f32[32,512]{1,0:T(8,128)S(1)} copy-done((f32[32,512]{1,0:T(8,128)S(1)}, f32[32,512]{1,0:T(8,128)}, u32[]{:S(2)}) %copy-start.5) | copy-done | bytes 65560
  8.6 0.0 copy-start.6
  8.6 0.7 %copy-done.6 = s32[4096]{0:T(1024)S(1)} copy-done((s32[4096]{0:T(1024)S(1)}, s32[4096]{0:T(1024)}, u32[]{:S(2)}) %copy-start.6) | copy-done | bytes 16408
  9.3 0.7 %copy-done.7 = s32[256]{0:T(256)S(1)} copy-done((s32[256]{0:T(256)S(1)}, s32[256]{0:T(256)}, u32[]{:S(2)}) %copy-start.7) | copy-done | bytes 1048
  10.0 0.0 copy-start.8
  10.0 0.7 %copy-done.8 = s32[32]{0:T(128)S(1)} copy-done((s32[32]{0:T(128)S(1)}, s32[32]{0:T(128)}, u32[]{:S(2)}) %copy-start.8) | copy-done | bytes 152
  10.6 0.0 copy-start.9
  10.6 0.7 %copy-done.9 = s32[32]{0:T(128)S(1)} copy-done((s32[32]{0:T(128)S(1)}, s32[32]{0:T(128)}, u32[]{:S(2)}) %copy-start.9) | copy-done | bytes 152
  11.3 0.0 copy-start.10
  11.3 0.7 %copy-done.10 = s32[64]{0:T(128)S(1)} copy-done((s32[64]{0:T(128)S(1)}, s32[64]{0:T(128)}, u32[]{:S(2)}) %copy-start.10) | copy-done | bytes 280
  12.0 19.2 %shard_map.122 = (f32[32,128]{1,0:T(8,128)S(1)}, f32[1,9]{1,0:T(1,128)S(1)}) custom-call(f32[8,4096]{1,0:T(8,128)S(1)} %copy-done.3, s32[32,128]{1,0:T(8,128)S(1)} %bitcast.3, f32[32,4096]{1,0:T(8,128)S(1)} %copy-done.1, f32[32,512]{1,0:T(8,128)S(1)} %copy-done.4, f32[32,512]{1,0:T(8,128)S(1)} %copy-done.5, f32[32,2048]{1,0:T(8,128)S(1)} %copy-done.2, ...), custom_call_target="tpu_custom_call" | custom-call | flops 20000000 | bytes 10000000 | tf_op jit(solution)/shard_map/pallas_call | solution.py:350
  31.2 0.6 %copy.15 = f32[4096]{0:T(1024)} copy(f32[4096]{0:T(1024)S(1)} %bitcast.4) | data formatting | bytes 32768
  31.8 0.5 %copy.16 = f32[9]{0:T(128)} copy(f32[9]{0:T(128)S(1)} %bitcast.5) | data formatting | bytes 72
  (1 shorter events, 0.0 us)
Async XLA Ops:
  0.6 3.4 %copy-start = (f32[32,256,256]{2,1,0:T(8,128)S(1)}, f32[32,256,256]{2,1,0:T(8,128)}, u32[]{:S(2)}) copy-start(f32[32,256,256]{2,1,0:T(8,128)} %nb_h.1) | copy-start | bytes 25165828
  4.0 1.0 %copy-start.1 = (f32[32,4096]{1,0:T(8,128)S(1)}, f32[32,4096]{1,0:T(8,128)}, u32[]{:S(2)}) copy-start(f32[32,4096]{1,0:T(8,128)} %basis_h.1) | copy-start | bytes 1572868
  5.1 0.9 %copy-start.2 = (f32[32,2048]{1,0:T(8,128)S(1)}, f32[32,2048]{1,0:T(8,128)}, u32[]{:S(2)}) copy-start(f32[32,2048]{1,0:T(8,128)} %far_h.1) | copy-start | bytes 786436
  6.0 0.9 %copy-start.3 = (f32[8,4096]{1,0:T(8,128)S(1)}, f32[8,4096]{1,0:T(8,128)}, u32[]{:S(2)}) copy-start(f32[8,4096]{1,0:T(8,128)} %kry_h.1) | copy-start | bytes 393220
  6.9 0.8 %copy-start.4 = (f32[32,512]{1,0:T(8,128)S(1)}, f32[32,512]{1,0:T(8,128)}, u32[]{:S(2)}) copy-start(f32[32,512]{1,0:T(8,128)} %trans_h.1) | copy-start | bytes 196612
  7.8 0.8 %copy-start.5 = (f32[32,512]{1,0:T(8,128)S(1)}, f32[32,512]{1,0:T(8,128)}, u32[]{:S(2)}) copy-start(f32[32,512]{1,0:T(8,128)} %top_h.1) | copy-start | bytes 196612
  8.6 0.7 %copy-start.6 = (s32[4096]{0:T(1024)S(1)}, s32[4096]{0:T(1024)}, u32[]{:S(2)}) copy-start(s32[4096]{0:T(1024)} %param.12) | copy-start | bytes 49156
  9.3 0.7 %copy-start.7 = (s32[256]{0:T(256)S(1)}, s32[256]{0:T(256)}, u32[]{:S(2)}) copy-start(s32[256]{0:T(256)} %owner_s.1) | copy-start | bytes 3076
  10.0 0.7 %copy-start.8 = (s32[32]{0:T(128)S(1)}, s32[32]{0:T(128)}, u32[]{:S(2)}) copy-start(s32[32]{0:T(128)} %nsrc_s.1) | copy-start | bytes 388
  10.6 0.7 %copy-start.9 = (s32[32]{0:T(128)S(1)}, s32[32]{0:T(128)}, u32[]{:S(2)}) copy-start(s32[32]{0:T(128)} %ntgt_s.1) | copy-start | bytes 388
  11.3 0.7 %copy-start.10 = (s32[64]{0:T(128)S(1)}, s32[64]{0:T(128)}, u32[]{:S(2)}) copy-start(s32[64]{0:T(128)} %fsrc_s.1) | copy-start | bytes 772

commit v2 on v1

--- a/solution.py
+++ b/solution.py
@@ -41,18 +41,22 @@
 def kernel(
     ndev, leaves, total,
     kry_h, perm_h, basis_h, trans_h, top_h, far_h, nb_h,
-    owner_s, nsrc_s, ntgt_s, fsrc_s,
-    out_ref, coef_ref,
-    kry, perm, basis, trans, top, far, nb,
+    owner_h, nsrc_h, ntgt_h, fsrc_h,
+    out_ref,
+    kry, perm, basis, trans, top, far, nb, owner_s, nsrc_s, ntgt_s, fsrc_s,
     x32, oh, xown, xin1, xin2, xin3, land1, land2, rolled, idx, ybuf,
     lsem, nsem, xsend, xrecv, s1, r1, s2, r2,
 ):
     me = lax.axis_index("leaf")
     chunks = leaves * 2
     groups = leaves // 4
+    shift = leaves.bit_length() - 1
+
+    def wrap(i):
+        return jnp.where(i >= ndev, i - ndev, i)
 
     def peer(k):
-        return {"leaf": lax.rem(me + k, ndev)}
+        return {"leaf": wrap(me + k)}
 
     def local(i, src, dst):
         return pltpu.make_async_copy(src, dst, lsem.at[i])
@@ -60,14 +64,15 @@
     loads = [
         local(i, s, d)
         for i, (s, d) in enumerate(
-            ((kry_h, kry), (perm_h, perm), (basis_h, basis), (trans_h, trans), (top_h, top), (far_h, far))
+            ((kry_h, kry), (perm_h, perm), (basis_h, basis), (trans_h, trans), (top_h, top), (far_h, far),
+             (owner_h, owner_s), (nsrc_h, nsrc_s), (ntgt_h, ntgt_s), (fsrc_h, fsrc_s))
         )
     ]
     near = [
         pltpu.make_async_copy(nb_h.at[pl.ds(g * CAP, CAP)], nb.at[pl.ds(g * CAP, CAP)], nsem.at[g])
         for g in range(4)
     ]
-    for cp in loads[:4]:
+    for cp in loads[:3]:
         cp.start()
     barrier = pltpu.get_barrier_semaphore()
 
@@ -78,7 +83,7 @@
     lax.fori_loop(1, ndev, greet, 0)
     for cp in near:
         cp.start()
-    for cp in loads[4:]:
+    for cp in loads[3:]:
         cp.start()
 
     sub8 = iota((8, LANES), 0)
@@ -112,7 +117,7 @@
             dst_ref=xbufs[g],
             send_sem=xsend.at[g],
             recv_sem=xrecv.at[g],
-            device_id=peer(hop + ndev),
+            device_id=peer(hop % ndev),
             device_id_type=MESH,
         )
         for g, hop in ((1, 1), (2, -1), (3, 2))
@@ -136,7 +141,7 @@
         row = rowsum(acc)
         qacc = qacc + trans[:, t * LANES : (t + 1) * LANES] * row
         tile = jnp.where(sub8 == t, row, tile)
-    qrow = rowsum(jnp.where(lane32 % K == sub32, lanesum(qacc), 0.0))
+    qrow = rowsum(jnp.where((lane32 & (K - 1)) == sub32, lanesum(qacc), 0.0))
     land1[me] = jnp.where(sub8 == groups, qrow, tile)
 
     def send1(k):
@@ -150,7 +155,7 @@
         )
 
     def recv1(k):
-        src = lax.rem(me - k + ndev, ndev)
+        src = wrap(me - k + ndev)
         return pltpu.make_async_remote_copy(
             src_ref=land1.at[src],
             dst_ref=land1.at[src],
@@ -166,6 +171,8 @@
 
     lax.fori_loop(1, ndev, start1, 0)
 
+    for cp in loads[6:]:
+        cp.wait()
     rows = iota((leaves, M), 0)
     sub16 = iota((16, M), 0)
     yc = jnp.zeros((leaves, M), F32)
@@ -177,7 +184,7 @@
         def slot(i, yc):
             n = g * CAP + i
             src = nsrc_s[n]
-            loc = lax.rem(owner_s[jnp.maximum(src, 0)], leaves)
+            loc = owner_s[jnp.maximum(src, 0)] & (leaves - 1)
             x = xbufs[g][pl.ds(loc, 1), :]
             xh = x.astype(BF16).astype(F32)
             lhs = jnp.where(sub16 == 0, xh, jnp.where(sub16 == 1, x - xh, 0.0)).astype(BF16)
@@ -198,15 +205,14 @@
         for i in range(chunks):
             part = kry[:, i * LANES : (i + 1) * LANES]
             acc = acc + part * kry[k : k + 1, i * LANES : (i + 1) * LANES]
-        gram = gram + jnp.where(lane8 % J == k, lanesum(acc), 0.0)
-    message = jnp.where(lane8 // J == sub8, gram, 0.0)
+        gram = gram + jnp.where((lane8 & (J - 1)) == k, lanesum(acc), 0.0)
+    message = jnp.where((lane8 >> 3) == sub8, gram, 0.0)
 
     stride = ndev * 8
     for i in range(leaves * NF):
         s = owner_s[fsrc_s[i]]
-        c = lax.rem(s, leaves)
-        turn = (i % NF - c) & 3
-        idx[i] = turn * stride + (s // leaves) * 8 + c // 4
+        turn = (i % NF - s) & 3
+        idx[i] = turn * stride + (s >> shift) * 8 + ((s & (leaves - 1)) >> 2)
 
     def wait1(k, _):
         recv1(k).wait_recv()
@@ -225,29 +231,29 @@
         row = jnp.zeros((1, LANES), F32)
         for ee in range(4):
             e = 4 * t + ee
-            row = row + jnp.where((lane1 // K == ee) & (me != e), land1[e, groups : groups + 1, :], 0.0)
+            row = row + jnp.where(((lane1 >> 5) == ee) & (me != e), land1[e, groups : groups + 1, :], 0.0)
         gacc = gacc + top[:, t * LANES : (t + 1) * LANES] * row
     gcol = lanesum(gacc)
 
-    y3 = jnp.zeros((3 * chunks, LANES), F32)
+    y3 = jnp.zeros((2 * chunks, LANES), F32)
     for c in range(leaves):
         t, cc = c // 4, c % 4
         if cc == 0:
             grow = rowsum(trans[:, t * LANES : (t + 1) * LANES] * gcol)
         r = jnp.zeros((1, LANES), F32)
         for f in range(NF):
-            r = jnp.where(lane1 // K == f, rolled[pl.ds(idx[c * NF + f], 1), :], r)
+            r = jnp.where((lane1 >> 5) == f, rolled[pl.ds(idx[c * NF + f], 1), :], r)
         acc = far[:, c * LANES : (c + 1) * LANES] * r + jnp.where(lane32 == cc * K + sub32, grow, 0.0)
         g = lanesum(acc)
-        for half in range(2):
-            i = 2 * c + half
-            yrow = yc[c : c + 1, half * LANES : (half + 1) * LANES] + rowsum(basis[:, i * LANES : (i + 1) * LANES] * g)
-            hit = iota((chunks, LANES), 0) == perm[i : i + 1, :] >> 7
-            lhs = jnp.concatenate([jnp.where(hit, v.astype(F32), 0.0).astype(BF16) for v in split3(yrow)], axis=0)
-            y3 = y3 + lax.dot_general(
-                lhs, oh[:, i * LANES : (i + 1) * LANES], (((1,), (1,)), ((), ())), preferred_element_type=F32
-            )
-    y = y3[:chunks] + y3[chunks : 2 * chunks] + y3[2 * chunks :]
+        yrow = yc[c : c + 1, :] + rowsum(basis[:, c * M : (c + 1) * M] * g)
+        hi = jnp.concatenate([perm[2 * c : 2 * c + 1, :], perm[2 * c + 1 : 2 * c + 2, :]], axis=1) >> 7
+        hit = iota((chunks, M), 0) == hi
+        top_half = yrow.astype(BF16).astype(F32)
+        lhs = jnp.concatenate([jnp.where(hit, v, 0.0).astype(BF16) for v in (top_half, yrow - top_half)], axis=0)
+        y3 = y3 + lax.dot_general(
+            lhs, oh[:, c * M : (c + 1) * M], (((1,), (1,)), ((), ())), preferred_element_type=F32
+        )
+    y = y3[:chunks] + y3[chunks:]
     ybuf[...] = y
 
     acc = jnp.zeros((8, LANES), F32)
@@ -271,7 +277,7 @@
         )
 
     def recv2(k):
-        src = lax.rem(me - k + ndev, ndev)
+        src = wrap(me - k + ndev)
         return pltpu.make_async_remote_copy(
             src_ref=land2.at[src],
             dst_ref=land2.at[src],
@@ -308,13 +314,14 @@
     h = (0.5 * kx + ky) * (1.0 / total)
     is_x = iota((8, 1), 0) == J - 1
     d = h - jnp.where(is_x, 0.5, 0.0)
-    left = rowsum(jnp.where(lane8 // J == sub8, d, 0.0))
-    right = rowsum(jnp.where(lane8 % J == sub8, d, 0.0))
+    left = rowsum(jnp.where((lane8 >> 3) == sub8, d, 0.0))
+    right = rowsum(jnp.where((lane8 & (J - 1)) == sub8, d, 0.0))
     along = rowsum(jnp.where(lane8 == 64 + sub8, -2.0 * d, 0.0))
     terms = sums * (left * right + along + jnp.where(lane1 == 72, 1.0, 0.0))
     squares = jnp.maximum(lanesum(terms), 0.0) * (1.0 / total)
     beta = jnp.sqrt(squares + 1e-06)
-    coef_ref[...] = (rowsum(jnp.where(lane8 == sub8, h, 0.0)) + jnp.where(lane1 == J, beta, 0.0))[:, : J + 1]
+    coef = rowsum(jnp.where(lane8 == sub8, h, 0.0)) + jnp.where(lane1 == J, beta, 0.0)
+    out_ref[chunks:, :] = jnp.where(sub8 == 0, coef, 0.0)
     for i in range(chunks):
         out_ref[i : i + 1, :] = (ybuf[i : i + 1, :] - rowsum(kry[:, i * LANES : (i + 1) * LANES] * d)) / beta
 
@@ -323,6 +330,11 @@
         return 0
 
     lax.fori_loop(1, ndev, sent2, 0)
+
+
+def take_apart(both_ref, nxt_ref, coef_ref):
+    nxt_ref[...] = both_ref[: nxt_ref.shape[0], :]
+    coef_ref[...] = both_ref[nxt_ref.shape[0] : nxt_ref.shape[0] + 1, : J + 1]
 
 
 def on_device(
@@ -342,20 +354,18 @@
     local_rows = tree_perm.shape[0]
     leaves = local_rows // M
     chunks = local_rows // LANES
-    hbm = pl.BlockSpec(memory_space=pl.ANY)
-    smem = pl.BlockSpec(memory_space=pltpu.SMEM)
+    hbm = pl.BlockSpec(memory_space=pltpu.HBM)
     vmem = pl.BlockSpec(memory_space=pltpu.VMEM)
     arrays = (krylov, tree_perm.reshape(chunks, LANES), basis, transfer, top_coup, far_coup, near_blocks)
+    indices = (owner, near_src, near_tgt, far_src)
     dma = pltpu.SemaphoreType.DMA
-    nxt, coeffs = pl.pallas_call(
+    both = pl.pallas_call(
         functools.partial(kernel, ndev, leaves, float(local_rows * ndev)),
-        out_shape=(
-            jax.ShapeDtypeStruct((chunks, LANES), F32),
-            jax.ShapeDtypeStruct((1, J + 1), F32),
-        ),
-        in_specs=[hbm] * 7 + [smem] * 4,
-        out_specs=(vmem, vmem),
+        out_shape=jax.ShapeDtypeStruct((chunks + 8, LANES), F32),
+        in_specs=[hbm] * 11,
+        out_specs=vmem,
         scratch_shapes=[pltpu.VMEM(a.shape, a.dtype) for a in arrays]
+        + [pltpu.SMEM(a.shape, a.dtype) for a in indices]
         + [
             pltpu.VMEM((chunks, LANES), F32),
             pltpu.VMEM((LANES, local_rows), BF16),
@@ -368,7 +378,7 @@
             pltpu.VMEM((4 * ndev * 8, LANES), F32),
             pltpu.SMEM((leaves * NF,), jnp.int32),
             pltpu.VMEM((chunks, LANES), F32),
-            dma((6,)),
+            dma((10,)),
             dma((4,)),
             dma((4,)),
             dma((4,)),
@@ -378,10 +388,19 @@
             dma((ndev,)),
         ],
         compiler_params=pltpu.CompilerParams(
-            collective_id=0, has_side_effects=True, vmem_limit_bytes=40 * 1024 * 1024
+            collective_id=0, has_side_effects=True, vmem_limit_bytes=60 * 1024 * 1024
         ),
         cost_estimate=pl.CostEstimate(flops=20_000_000, bytes_accessed=10_000_000, transcendentals=0),
-    )(*arrays, owner, near_src, near_tgt, far_src)
+    )(*arrays, *indices)
+    nxt, coeffs = pl.pallas_call(
+        take_apart,
+        out_shape=(
+            jax.ShapeDtypeStruct((chunks, LANES), F32),
+            jax.ShapeDtypeStruct((1, J + 1), F32),
+        ),
+        in_specs=[vmem],
+        out_specs=(vmem, vmem),
+    )(both)
     return nxt.reshape(local_rows), coeffs.reshape(J + 1)
 
 

time: 32.8 us -> 20.2 us (0.62)
  local copies, waits for them, and re-layouts: 12.4 us -> 0 us
    unnamed x24 -> x0, local copies, waits for them, and re-layouts: 12.4 us -> none
    pallas_call x0 -> x1, Pallas kernels: none -> 1.34 us  [on_device(): pl.pallas_call(take_apart, out_shape=(jax.ShapeDtypeStruct((chunks, LANES...]
    pallas_call x1, Pallas kernels: 19.2 us -> 18 us  [on_device(): pl.pallas_call(functools.partial(kernel, ndev, leaves, float(local_rows *...]
where the time goes in v2:
time: 20.2 us; the launch traced here: 20 us
  Pallas kernels  19.3 us (96%)
  between operations  0.64 us (3%)
    pallas_call x1, Pallas kernels, on_device(): pl.pallas_call(functools.partial(kernel, ndev, leaves, float(local_rows *...  18 us
    pallas_call x1, Pallas kernels, on_device(): pl.pallas_call(take_apart, out_shape=(jax.ShapeDtypeStruct((chunks, LANES...  1.34 us

profile of v2, /device:TPU:0, one launch (start us, length us, event | category | flops | bytes accessed | tf_op | source)
XLA Modules:
  0.0 20.0 jit_solution(9749884958337153258)
XLA Ops:
  0.6 18.0 %shard_map.122.both_ref = f32[40,128]{1,0:T(8,128)} custom-call(f32[8,4096]{1,0:T(8,128)} %kry_h.1, s32[32,128]{1,0:T(8,128)} %bitcast.3, f32[32,4096]{1,0:T(8,128)} %basis_h.1, f32[32,512]{1,0:T(8,128)} %trans_h.1, f32[32,512]{1,0:T(8,128)} %top_h.1, f32[32,2048]{1,0:T(8,128)} %far_h.1, f32[32,256,256]{2,1,0:T(8,128)} %nb_h.1, s32[256]{0:T(256)} %owner_h.1, ...), custom_call_target="tpu_custom_call" | custom-call | flops 20000000 | bytes 10000000 | tf_op jit(solution)/shard_map/pallas_call | solution.py:362
  18.6 1.3 %shard_map.123 = (f32[32,128]{1,0:T(8,128)}, f32[1,9]{1,0:T(1,128)}) custom-call(f32[40,128]{1,0:T(8,128)} %shard_map.122.both_ref), custom_call_target="tpu_custom_call" | custom-call | tf_op jit(solution)/shard_map/pallas_call | solution.py:395

commit v3 on v2

--- a/solution.py
+++ b/solution.py
@@ -107,23 +107,6 @@
         hi = perm[i : i + 1, :] >> 7
         half = (i % 2) * LANES
         xown[i // 2 : i // 2 + 1, half : half + LANES] = rowsum(jnp.where(iota((chunks, LANES), 0) == hi, a, 0.0))
-
-    pl.semaphore_wait(barrier, ndev - 1)
-
-    xbufs = (xown, xin1, xin2, xin3)
-    xcopies = [
-        pltpu.make_async_remote_copy(
-            src_ref=xown,
-            dst_ref=xbufs[g],
-            send_sem=xsend.at[g],
-            recv_sem=xrecv.at[g],
-            device_id=peer(hop % ndev),
-            device_id_type=MESH,
-        )
-        for g, hop in ((1, 1), (2, -1), (3, 2))
-    ]
-    for cp in xcopies:
-        cp.start()
 
     loads[2].wait()
     loads[3].wait()
@@ -144,6 +127,40 @@
     qrow = rowsum(jnp.where((lane32 & (K - 1)) == sub32, lanesum(qacc), 0.0))
     land1[me] = jnp.where(sub8 == groups, qrow, tile)
 
+    for cp in loads[6:]:
+        cp.wait()
+    gram = jnp.zeros((8, LANES), F32)
+    for k in range(J):
+        acc = jnp.zeros((8, LANES), F32)
+        for i in range(chunks):
+            part = kry[:, i * LANES : (i + 1) * LANES]
+            acc = acc + part * kry[k : k + 1, i * LANES : (i + 1) * LANES]
+        gram = gram + jnp.where((lane8 & (J - 1)) == k, lanesum(acc), 0.0)
+    message = jnp.where((lane8 >> 3) == sub8, gram, 0.0)
+
+    stride = ndev * 8
+    for i in range(leaves * NF):
+        s = owner_s[fsrc_s[i]]
+        turn = (i % NF - s) & 3
+        idx[i] = turn * stride + (s >> shift) * 8 + ((s & (leaves - 1)) >> 2)
+
+    pl.semaphore_wait(barrier, ndev - 1)
+
+    xbufs = (xown, xin1, xin2, xin3)
+    xcopies = [
+        pltpu.make_async_remote_copy(
+            src_ref=xown,
+            dst_ref=xbufs[g],
+            send_sem=xsend.at[g],
+            recv_sem=xrecv.at[g],
+            device_id=peer(hop % ndev),
+            device_id_type=MESH,
+        )
+        for g, hop in ((1, 1), (2, -1), (3, 2))
+    ]
+    for cp in xcopies:
+        cp.start()
+
     def send1(k):
         return pltpu.make_async_remote_copy(
             src_ref=land1.at[me],
@@ -171,8 +188,6 @@
 
     lax.fori_loop(1, ndev, start1, 0)
 
-    for cp in loads[6:]:
-        cp.wait()
     rows = iota((leaves, M), 0)
     sub16 = iota((16, M), 0)
     yc = jnp.zeros((leaves, M), F32)
@@ -198,21 +213,6 @@
             return yc + jnp.where(rows == tgt, r[0:1] + r[1:2], 0.0)
 
         yc = lax.fori_loop(0, CAP, slot, yc, unroll=True)
-
-    gram = jnp.zeros((8, LANES), F32)
-    for k in range(J):
-        acc = jnp.zeros((8, LANES), F32)
-        for i in range(chunks):
-            part = kry[:, i * LANES : (i + 1) * LANES]
-            acc = acc + part * kry[k : k + 1, i * LANES : (i + 1) * LANES]
-        gram = gram + jnp.where((lane8 & (J - 1)) == k, lanesum(acc), 0.0)
-    message = jnp.where((lane8 >> 3) == sub8, gram, 0.0)
-
-    stride = ndev * 8
-    for i in range(leaves * NF):
-        s = owner_s[fsrc_s[i]]
-        turn = (i % NF - s) & 3
-        idx[i] = turn * stride + (s >> shift) * 8 + ((s & (leaves - 1)) >> 2)
 
     def wait1(k, _):
         recv1(k).wait_recv()

time: 20.2 us -> 19.6 us (0.970)
  Pallas kernels: 19.3 us -> 18.8 us
    pallas_call x1, Pallas kernels: 18 us -> 17.4 us  [on_device(): pl.pallas_call(functools.partial(kernel, ndev, leaves, float(local_rows *...]
where the time goes in v3:
time: 19.6 us; the launch traced here: 19.4 us
  Pallas kernels  18.8 us (96%)
  between operations  0.64 us (3%)
    pallas_call x1, Pallas kernels, on_device(): pl.pallas_call(functools.partial(kernel, ndev, leaves, float(local_rows *...  17.4 us
    pallas_call x1, Pallas kernels, on_device(): pl.pallas_call(take_apart, out_shape=(jax.ShapeDtypeStruct((chunks, LANES...  1.34 us

profile of v3, /device:TPU:0, one launch (start us, length us, event | category | flops | bytes accessed | tf_op | source)
XLA Modules:
  0.0 19.4 jit_solution(10292300655258573417)
XLA Ops:
  0.6 17.4 %shard_map.122.both_ref = f32[40,128]{1,0:T(8,128)} custom-call(f32[8,4096]{1,0:T(8,128)} %kry_h.1, s32[32,128]{1,0:T(8,128)} %bitcast.3, f32[32,4096]{1,0:T(8,128)} %basis_h.1, f32[32,512]{1,0:T(8,128)} %trans_h.1, f32[32,512]{1,0:T(8,128)} %top_h.1, f32[32,2048]{1,0:T(8,128)} %far_h.1, f32[32,256,256]{2,1,0:T(8,128)} %nb_h.1, s32[256]{0:T(256)} %owner_h.1, ...), custom_call_target="tpu_custom_call" | custom-call | flops 20000000 | bytes 10000000 | tf_op jit(solution)/shard_map/pallas_call | solution.py:362
  18.1 1.3 %shard_map.123 = (f32[32,128]{1,0:T(8,128)}, f32[1,9]{1,0:T(1,128)}) custom-call(f32[40,128]{1,0:T(8,128)} %shard_map.122.both_ref), custom_call_target="tpu_custom_call" | custom-call | tf_op jit(solution)/shard_map/pallas_call | solution.py:395
